TPU v7x, 512 devices: a whole 4x8x8 slice. The times are simulated.
512 devices in a mesh: group: 8 (over z), mem: 64 (over x, y, core).
Axes of the slice: x: 4, y: 8, z: 8, core: 2. Of those that a mesh axis runs over, the one named last changes fastest.
Arguments:
- node_memory: float32 [8, 16384, 512], P('group', 'mem'), may hold values from -6 to 6
- batch_owner: int32 [8, 8192, 1], P('group', 'mem'), may hold values from 0 to 63; in each aligned block of 128 rows (0 to 127, 128 to 255, ..., all dimensions but the last counted through in order) at most 4 rows name the same one
- batch_row: int32 [8, 8192], P('group', 'mem'), may hold values from 0 to 255
- batch_time: int32 [8, 8192], P('group', 'mem'), may hold values from 4096 to 8191
- neighbour_owner: int32 [8, 81920, 1], P('group', 'mem'), may hold values from 0 to 63; in each aligned block of 1280 rows (0 to 1279, 1280 to 2559, ..., all dimensions but the last counted through in order) at most 40 rows name the same one
- neighbour_row: int32 [8, 81920], P('group', 'mem'), may hold values from 0 to 255
- neighbour_time: int32 [8, 81920], P('group', 'mem'), may hold values from 0 to 4095
- frequency: float32 [512], replicated, may hold values from 0.0001 to 0.03
- phase_shift: float32 [512], replicated, may hold values from -3.140625 to 3.140625
- w_message: bfloat16 [512, 512], replicated, may hold values from -0.25 to 0.25
- w_input: bfloat16 [512, 1536], replicated, may hold values from -0.25 to 0.25
- w_recur: bfloat16 [512, 1536], replicated, may hold values from -0.25 to 0.25
- cotangent: bfloat16 [8, 8192, 512], P('group', 'mem'), may hold values from -6 to 6
Outputs:
- new_memory: float32 [8, 16384, 512], P('group', 'mem')
- grad_input: float32 [512, 1536], P('mem')
Inputs may be any that keep to these rules, and one draw needn't show every extreme that they name: `batch_owner`: in each aligned block of 128 rows (the rows of one device) no owner is named by more than 4 rows, a bound that some block reaches. `neighbour_owner`: in each aligned block of 1280 rows (the rows of one device) no owner is named by more than 40 rows, a bound that some block reaches.
All inputs are finite; a program needn't handle non-finite values.
Results may differ from a plain program's by a relative error of at most 0.013.
Values may be sent and summed in bfloat16 or wider, within the bound.
A program may use at most 64 MiB of HBM per device.

v0:
```python
import math

import jax
import jax.numpy as jnp
from jax import lax
from jax.experimental import pallas as pl
from jax.experimental.pallas import tpu as pltpu
from jax.sharding import PartitionSpec as P

f32, bf16, i32 = jnp.float32, jnp.bfloat16, jnp.int32
MESH = pl.DeviceIdType.MESH

age_scale = 1024.0
X, Y, Z = 4, 8, 8
ROW = 2 * X
WIDTH = 512
NODE = 256
BATCH = 128
NBRS = 10
CAPN, CAPB = 40, 4
SLOT = CAPN + CAPB
BLOCK = ROW * SLOT
STEP = 32
NEAR = (0, 1, 7, 2, 6)
COS = (
    1.0,
    -19.73920440673828,
    64.93911743164062,
    -85.45014190673828,
    60.16762924194336,
    -25.967599868774414,
    6.528658390045166,
)


def inv_row(d):
    return ((-(d // 2)) % X) * 2 + d % 2


def inv_y(e):
    return (-e) % Y


def iota(shape, dim):
    return lax.broadcasted_iota(i32, shape, dim)


def mm(a, b):
    return lax.dot_general(a, b, (((1,), (0,)), ((), ())), preferred_element_type=f32)


def mm_nt(a, b):
    return lax.dot_general(a, b, (((1,), (1,)), ((), ())), preferred_element_type=f32)


def mm_tn(a, b):
    return lax.dot_general(a, b, (((0,), (0,)), ((), ())), preferred_element_type=f32)


def onehot(mask):
    return jnp.where(mask, 1.0, 0.0).astype(bf16)


def sigmoid(v):
    return 0.5 * jnp.tanh(0.5 * v) + 0.5


def kernel(
    bo_hbm, br_hbm, bt_hbm, no_hbm, nr_hbm, nt_hbm, freq_hbm, phase_hbm,
    node_hbm, wm_hbm, wi_hbm, wr_hbm, ct_hbm,
    out_mem, out_grad,
    bo, br, bt, no, nr, nt, freq, phase, meta_sem,
    node, wm, wi, wr, ct, load_sem,
    coltab, y_send, y_recv, o_send, o_recv,
    askbuf, askrecv, ask_send, ask_recv,
    far, far_send, far_recv,
    idbuf, idone, id_send, id_recv, idsum, idtwo, idx_send, idx_recv,
    codes, encos, parts, pick,
    sendbuf, slots, s_send, s_recv,
    agg, hid, tot,
    sel, tsc, perm,
    wbs, wb1, wb2, wx_send, wx_recv, wy_send, wy_recv,
    fact, dpre, c_send, c_recv,
    gx, gxr, gx_send, gx_recv,
    gy, gyr, gy_send, gy_recv,
    gz, gz_send, gz_recv,
):
    zi = lax.axis_index("group")
    me = lax.axis_index("mem")
    xi, yi, ci = me // 16, (me // 2) % Y, me % 2

    def at_row(d):
        return (zi, ((xi + d // 2) % X) * 16 + yi * 2 + (ci + d % 2) % 2)

    def at_y(e):
        return (zi, xi * 16 + ((yi + e) % Y) * 2 + ci)

    def at_z(g):
        return ((zi + g) % Z, me)

    def send(src, dst, ssem, rsem, to):
        copy = pltpu.make_async_remote_copy(
            src_ref=src, dst_ref=dst, send_sem=ssem, recv_sem=rsem, device_id=to, device_id_type=MESH
        )
        copy.start()
        sent.append(copy)

    def landed(dst, rsem):
        pltpu.make_async_remote_copy(
            src_ref=dst, dst_ref=dst, send_sem=rsem, recv_sem=rsem, device_id=at_y(1), device_id_type=MESH
        ).wait_recv()

    sent = []

    barrier = pltpu.get_barrier_semaphore()
    for d in range(1, ROW):
        pl.semaphore_signal(barrier, inc=1, device_id=at_row(d), device_id_type=MESH)
    for e in range(1, Y):
        pl.semaphore_signal(barrier, inc=1, device_id=at_y(e), device_id_type=MESH)
    for g in range(1, Z):
        pl.semaphore_signal(barrier, inc=1, device_id=at_z(g), device_id_type=MESH)
    small = [
        pltpu.make_async_copy(src, dst, meta_sem.at[i])
        for i, (src, dst) in enumerate(
            (
                (no_hbm, no), (nr_hbm, nr), (bo_hbm, bo), (br_hbm, br),
                (nt_hbm, nt), (bt_hbm, bt), (freq_hbm, freq), (phase_hbm, phase),
            )
        )
    ]
    loads = [
        pltpu.make_async_copy(src, dst, load_sem.at[i])
        for i, (src, dst) in enumerate(
            ((node_hbm, node), (wm_hbm, wm), (wi_hbm, wi), (wr_hbm, wr), (ct_hbm, ct))
        )
    ]
    for copy in small:
        copy.start()
    loads[0].start()
    for copy in small:
        copy.wait()

    def relative(owner):
        dx = (owner // 16 - xi) & (X - 1)
        dc = (owner - ci) & 1
        return dx, dc, (owner // 2 - yi) & (Y - 1)

    dx_n, dc_n, re_n = relative(no[...])
    dx_b, dc_b, re_b = relative(bo[...])
    rd_b = dx_b * 2 + dc_b

    def lanes_of(near, core):
        return [near[:, j * BATCH : (j + 1) * BATCH] for j in range(NBRS)] + [core]

    owner_at = lanes_of((dx_n * 2 + dc_n) * Y + re_n, rd_b * Y + re_b)
    chip_at = lanes_of(dx_n * Y + re_n, dx_b * Y + re_b)
    hot = [onehot(iota((64, BATCH), 0) == o) for o in owner_at]
    before = onehot(iota((BATCH, 2 * BATCH), 0) < iota((BATCH, 2 * BATCH), 1))
    counts = mm(jnp.concatenate(hot, axis=0), before)
    run = jnp.zeros((64, BATCH), f32)
    ranks = []
    for j in range(NBRS + 1):
        part = counts[j * 64 : (j + 1) * 64]
        prior = part[:, :BATCH] + run if j < NBRS else part[:, :BATCH]
        ranks.append(jnp.sum(hot[j].astype(f32) * prior, axis=0, keepdims=True).astype(i32))
        run = run + part[:, BATCH:]
    rank_b = ranks[NBRS]
    core_at = lanes_of(dc_n, dc_b)
    position = [
        core_at[j] * SLOT + ranks[j] + (CAPN if j == NBRS else 0) for j in range(NBRS + 1)
    ]
    chips = jnp.concatenate([onehot(iota((X * Y, BATCH), 0) == o) for o in chip_at], axis=1)
    row_at = lanes_of(nr[...], br[...])
    near_at = iota((2 * SLOT, BATCH), 0)
    slot_at = iota((128, BATCH), 0)

    def placed(j, value):
        return jnp.where(slot_at == position[j], value.astype(f32), 0.0).astype(bf16)

    ask_rows = mm_nt(chips, jnp.concatenate([placed(j, row_at[j]) for j in range(NBRS + 1)], axis=1))
    for k in range(X):
        tile = ask_rows[k * Y : (k + 1) * Y]
        if k == 0:
            askrecv[0] = tile
        else:
            askbuf[k] = tile
    loads[0].wait()
    coltab[0, 0] = node[...].astype(bf16)
    pl.semaphore_wait(barrier, ROW + Y + Z - 3)

    sibling = at_row(1)
    half = NODE // 2

    def ring(e, to, step, h):
        rows = pl.ds(h * half, half)
        send(coltab.at[e, 0, rows], coltab.at[to, 0, rows], y_send.at[to, h], y_recv.at[to, h], at_y(step))

    def arrived(e, h):
        landed(coltab.at[e, 0, pl.ds(h * half, half)], y_recv.at[e, h])

    for k in (2, 1, 3):
        send(askbuf.at[k], askrecv.at[(-k) % X], ask_send.at[k], ask_recv.at[(-k) % X], at_row(2 * k))
    send(coltab.at[0, 0], coltab.at[0, 1], o_send.at[0], o_recv.at[0], sibling)
    for h in range(2):
        ring(0, Y - 1, 1, h)
        ring(0, 1, -1, h)
    send(coltab.at[0, 0], far.at[0], far_send.at[0], far_recv.at[0], at_row(4))

    wanted = ((slot_at & 3) == rank_b) & ((slot_at // 16) == ((0 - re_b) & (Y - 1)))
    id_rows = mm_nt(
        onehot(iota((64, BATCH), 0) == re_b * ROW + rd_b),
        jnp.where(wanted, br[...].astype(f32) + 1.0, 0.0).astype(bf16),
    )
    for e in range(Y):
        tile = jnp.concatenate([id_rows[e * ROW : (e + 1) * ROW], ask_rows[2 * Y : 3 * Y]], axis=0)
        if e == 0:
            idone[0] = tile
        else:
            idbuf[e] = tile
            send(idbuf.at[e], idone.at[inv_y(e)], id_send.at[e], id_recv.at[inv_y(e)], at_y(e))

    for k in range(1, X):
        landed(askrecv.at[k], ask_recv.at[k])
    asks = askrecv[...]
    eye = onehot(iota((2 * SLOT, 128), 0) == iota((2 * SLOT, 128), 1))
    ask_cols = mm_nt(eye, asks.reshape(X * Y, 128).astype(bf16)).astype(i32)
    ask_cols = ask_cols + jnp.where(iota((2 * SLOT, X * Y), 0) >= SLOT, NODE, 0)

    def hand_on(e):
        send(coltab.at[e, 0], coltab.at[e, 1], o_send.at[e], o_recv.at[e], sibling)

    def serve(e):
        landed(coltab.at[e, 1], o_recv.at[e])
        lanes = iota((2 * SLOT, 2 * NODE), 1)
        both = coltab[e].reshape(2 * NODE, WIDTH)
        for k in (2, 1, 3, 0):
            if k == 2 and e in NEAR:
                continue
            hit = onehot(ask_cols[:, k * Y + e : k * Y + e + 1] == lanes)
            rows = mm(hit, both)
            rows = jnp.concatenate([rows[:, :256], rows[:, 256:]], axis=0).astype(bf16)
            if k == 0:
                slots[e, 0] = rows
            else:
                sendbuf[e, k] = rows
                send(
                    sendbuf.at[e, k], slots.at[e, (-k) % X],
                    s_send.at[e, k], s_recv.at[e, (-k) % X], at_row(2 * k),
                )

    def serve_far():
        landed(far.at[1], far_recv.at[1])
        far_asks = jnp.concatenate([idone[f, ROW : 2 * ROW] for f in NEAR], axis=0).astype(bf16)
        far_cols = mm_nt(eye, far_asks).astype(i32)
        far_cols = far_cols + jnp.where(iota(far_cols.shape, 0) >= SLOT, NODE, 0)
        lanes = iota((2 * SLOT, 2 * NODE), 1)
        both = far[...].reshape(2 * NODE, WIDTH)
        for i, f in enumerate(NEAR):
            column = 8 * i + inv_y(f)
            rows = mm(onehot(far_cols[:, column : column + 1] == lanes), both)
            rows = jnp.concatenate([rows[:, :256], rows[:, 256:]], axis=0).astype(bf16)
            if f == 0:
                slots[0, 2] = rows
            else:
                sendbuf[f, 2] = rows
                send(
                    sendbuf.at[f, 2], slots.at[inv_y(f), 2],
                    s_send.at[f, 2], s_recv.at[inv_y(f), 2], at_y(f),
                )

    def prepare(e):
        def one(i, carry):
            rows = pl.ds(pl.multiple_of(i * STEP, STEP), STEP)
            code = codes[e, rows].astype(i32)
            here = (code >> 12) == iota((STEP, BATCH), 1) + 1
            age = jnp.where(here, (bt[...] - (code & 4095)).astype(f32), 0.0)
            weight = jnp.where(here, 1.0 / (1.0 + age / age_scale), 0.0)
            high = weight.astype(bf16)
            low = (weight - high.astype(f32)).astype(bf16)
            parts[e, rows] = jnp.concatenate([high, low], axis=1)
            pick[e, rows] = onehot(iota((STEP, BATCH), 0) + (e * BLOCK + i * STEP) == slot_b)
            age = jnp.sum(age, axis=1, keepdims=True)
            turns = age * (freq[...] * (0.5 / math.pi)) + phase[...] * (0.5 / math.pi)
            turns = turns - jnp.floor(turns + 0.5)
            square = turns * turns
            value = jnp.full((STEP, WIDTH), COS[-1], f32)
            for c in COS[-2::-1]:
                value = value * square + c
            encos[e, rows] = value
            return carry

        lax.fori_loop(0, BLOCK // STEP, one, 0, unroll=True)
        ones = jnp.ones((BLOCK, 128), bf16)
        part = mm_tn(parts[e], ones)
        part = part[:BATCH] + part[BATCH:]
        if e == 0:
            tot[...] = part
        else:
            tot[...] += part

    def fold(e):
        for k in range(1, X):
            if e or k != 2:
                landed(slots.at[e, k], s_recv.at[e, k])
        got = [slots[e, k].astype(f32) for k in range(X)]
        got = jnp.concatenate(
            [jnp.concatenate([g[: 2 * SLOT], g[2 * SLOT :]], axis=1) for g in got], axis=0
        )
        enc = (got + encos[e]).astype(bf16)
        pre = mm(enc, wm[...])
        msg = (pre * sigmoid(pre)).astype(bf16)
        part = mm_tn(parts[e], msg)
        part = part[:BATCH] + part[BATCH:]
        mem = mm_tn(pick[e], got.astype(bf16))
        if e == 0:
            agg[...] = part
            hid[...] = mem
        else:
            agg[...] += part
            hid[...] += mem

    serve(0)
    for load in loads[1:]:
        load.start()

    number = (iota((1, NBRS * BATCH), 1) * 6554) >> 16
    times = nt[...]
    values = [
        jnp.concatenate(
            [
                jnp.where(
                    near_at == position[j], value[:, j * BATCH : (j + 1) * BATCH].astype(f32), 0.0
                ).astype(bf16)
                for j in range(NBRS)
            ],
            axis=1,
        )
        for value in (number + 1, times >> 6, times & 63)
    ]
    near_chips = chips[:, : NBRS * BATCH]
    table = mm_nt(values[0], near_chips) * 4096.0
    table = table + mm_nt(values[1], near_chips) * 64.0 + mm_nt(values[2], near_chips)
    for e in range(Y):
        for k in range(X):
            column = table[:, k * Y + e : k * Y + e + 1]
            codes[e, k * 2 * SLOT : (k + 1) * 2 * SLOT] = jnp.broadcast_to(column, (2 * SLOT, BATCH))
    slot_b = re_b * BLOCK + dx_b * (2 * SLOT) + position[NBRS]


    def pass_on(e, h):
        for e, step in ((Y - e, 1), (e, -1)):
            arrived(e, h)
            if e not in (3, Y - 3) or (e == Y - 3) == (h == 0):
                ring(e, (e - step) % Y, step, h)

    prepare(0)
    pass_on(1, 0)
    pass_on(1, 1)
    hand_on(Y - 1)
    hand_on(1)
    serve(Y - 1)
    serve(1)
    prepare(Y - 1)
    pass_on(2, 0)
    prepare(1)
    pass_on(2, 1)
    hand_on(Y - 2)
    hand_on(2)
    serve(Y - 2)
    serve(2)
    landed(far.at[0], far_recv.at[0])
    send(far.at[0], far.at[1], far_send.at[1], far_recv.at[1], sibling)

    for e in range(1, Y):
        landed(idone.at[e], id_recv.at[e])
    ids = idone[0, 0:ROW]
    for e in range(1, Y):
        ids = ids + idone[e, 0:ROW]
    idsum[...] = ids
    for d in range(1, ROW):
        send(idsum, idtwo.at[inv_row(d)], idx_send.at[d], idx_recv.at[inv_row(d)], at_row(d))

    pass_on(3, 0)
    prepare(Y - 2)
    pass_on(3, 1)
    hand_on(Y - 3)
    hand_on(3)
    serve(Y - 3)
    serve(3)
    prepare(2)
    prepare(Y - 3)
    arrived(4, 0)
    arrived(4, 1)
    hand_on(4)
    serve_far()
    serve(4)

    prepare(3)
    prepare(4)
    loads[1].wait()
    for e in (0, Y - 1, 1, Y - 2, 2):
        fold(e)

    target = re_b * 128 + rd_b * 16 + rank_b
    target = jnp.concatenate([target + 4 * q for q in range(4)], axis=1)
    sel[...] = onehot(iota((Y * 128, 4 * BATCH), 0) == target)
    place = iota((1, 256), 1)
    wanted_row = ((xi + place // 64) & (X - 1)) * 128 + ((yi + (place // 8) % Y) & (Y - 1)) * 16 + (place & 7)
    for s in range(2):
        perm[s] = onehot(iota((WIDTH, 256), 0) == wanted_row + ((ci + s) & 1) * 8)
    for e in (Y - 3, 3, 4):
        fold(e)

    for load in loads[2:]:
        load.wait()
    scale = 1.0 / tot[...]
    agg_bf = (agg[...] * jnp.concatenate([scale] * 4, axis=1)).astype(bf16)
    fact[1, 0:BATCH] = mm(agg_bf, perm[1]).astype(bf16)
    send(fact.at[1, pl.ds(0, BATCH)], fact.at[0, pl.ds(BATCH, BATCH)], c_send.at[0], c_recv.at[0], sibling)
    fact[0, 0:BATCH] = mm(agg_bf, perm[0]).astype(bf16)
    hidden = hid[...]
    hid_bf = hidden.astype(bf16)

    def cols(ref, g):
        return ref[:, g * WIDTH : (g + 1) * WIDTH]

    recur = mm(hid_bf, cols(wr, 2))
    reset = sigmoid(mm(agg_bf, cols(wi, 1)) + mm(hid_bf, cols(wr, 1)))
    candidate = jnp.tanh(mm(agg_bf, cols(wi, 2)) + reset * recur)
    update = sigmoid(mm(agg_bf, cols(wi, 0)) + mm(hid_bf, cols(wr, 0)))
    up = ct[...].astype(f32)
    d_cand = up * update * (1.0 - candidate * candidate)
    d_reset = d_cand * recur * reset * (1.0 - reset)
    gap = candidate - hidden
    d_update = up * gap * update * (1.0 - update)
    for g, part in enumerate((d_update, d_reset, d_cand)):
        dpre[g, 0:BATCH] = part.astype(bf16)
        send(
            dpre.at[g, pl.ds(0, BATCH)], dpre.at[g, pl.ds(BATCH, BATCH)],
            c_send.at[1 + g], c_recv.at[1 + g], sibling,
        )

    change = (update * gap).astype(bf16)
    change = jnp.concatenate([change[:, q * 128 : (q + 1) * 128] for q in range(4)], axis=0)
    packed = mm(sel[...], change).astype(bf16).reshape(Y, ROW, 16, 128)
    wbs[...] = packed
    wb1[:, 0] = packed[0]
    for e in (4, 3, 5, 2, 6, 1, 7):
        send(wbs.at[e], wb1.at[:, inv_y(e)], wy_send.at[e], wy_recv.at[inv_y(e)], at_y(e))

    landed(fact.at[0, pl.ds(BATCH, BATCH)], c_recv.at[0])
    mine = []
    for g in range(3):
        landed(dpre.at[g, pl.ds(BATCH, BATCH)], c_recv.at[1 + g])
        grad = mm_tn(fact[0], dpre[g])
        mine.append(grad[0:64])
        gx[g] = grad[64:256].astype(bf16)
        for k in (2, 1, 3):
            send(
                gx.at[g, pl.ds((k - 1) * 64, 64)], gxr.at[g, (-k) % X],
                gx_send.at[g, k], gx_recv.at[g, (-k) % X], at_row(2 * k),
            )

    for d in range(ROW):
        if d == 0:
            line = idsum[0:1]
        else:
            landed(idtwo.at[d], idx_recv.at[d])
            line = idtwo[d, inv_row(d) : inv_row(d) + 1]
        tsc[:, d * 128 : (d + 1) * 128] = onehot(iota((NODE, 128), 0) + 1 == line.astype(i32))

    own = []
    for g in range(3):
        acc = mine[g]
        for k in range(1, X):
            landed(gxr.at[g, k], gx_recv.at[g, k])
            acc = acc + gxr[g, k].astype(f32)
        own.append(acc[0:8])
        left, right = acc[:, 0:256], acc[:, 256:512]
        for e in (4, 3, 5, 2, 6, 1, 7):
            rows = slice(e * 8, e * 8 + 8)
            gy[g, e] = jnp.concatenate([left[rows], right[rows]], axis=0).astype(bf16)
            send(gy.at[g, e], gyr.at[g, inv_y(e)], gy_send.at[g, e], gy_recv.at[g, inv_y(e)], at_y(e))

    for e in range(1, Y):
        landed(wb1.at[:, e], wy_recv.at[e])
    for d in (4, 5, 2, 3, 6, 7, 1):
        send(wb1.at[d], wb2.at[inv_row(d)], wx_send.at[d], wx_recv.at[inv_row(d)], at_row(d))
    wb2[0] = wb1[0]

    for g in range(3):
        acc = jnp.concatenate([own[g][:, 0:256], own[g][:, 256:512]], axis=0)
        for e in range(1, Y):
            landed(gyr.at[g, e], gy_recv.at[g, e])
            acc = acc + gyr[g, e].astype(f32)
        gz[g, zi] = acc.astype(bf16)
        for k in (4, 3, 5, 2, 6, 1, 7):
            send(gz.at[g, zi], gz.at[g, zi], gz_send.at[g, k], gz_recv.at[g, (-k) % Z], at_z(k))

    for d in range(1, ROW):
        landed(wb2.at[d], wx_recv.at[d])
    back = wb2[...].reshape(ROW * 128, 128)
    quarter = (iota((ROW * 128, 128), 0) // 4) & 3
    wide = jnp.concatenate(
        [jnp.where(quarter == q, back.astype(f32), 0.0).astype(bf16) for q in range(4)], axis=1
    )
    out_mem[...] = mm(tsc[...], wide)

    for g in range(3):
        for k in range(1, Z):
            landed(gz.at[g, (zi + k) % Z], gz_recv.at[g, k])
        for h in range(2):
            acc = gz[g, 4 * h].astype(f32)
            for k in range(1, 4):
                acc = acc + gz[g, 4 * h + k].astype(f32)
            out_grad[h, :, g * WIDTH : g * WIDTH + 256] = acc[0:8]
            out_grad[h, :, g * WIDTH + 256 : (g + 1) * WIDTH] = acc[8:16]

    for copy in sent:
        copy.wait_send()


def body(
    node_memory, batch_owner, batch_row, batch_time, neighbour_owner, neighbour_row, neighbour_time,
    frequency, phase_shift, w_message, w_input, w_recur, cotangent,
):
    dma = pltpu.SemaphoreType.DMA
    vmem = pl.BlockSpec(memory_space=pltpu.VMEM)
    hbm = pl.BlockSpec(memory_space=pl.ANY)
    rows = NBRS * BATCH
    owned = node_memory.reshape(NODE, WIDTH)
    change, grad = pl.pallas_call(
        kernel,
        out_shape=(
            jax.ShapeDtypeStruct((NODE, WIDTH), f32),
            jax.ShapeDtypeStruct((2, 8, 3 * WIDTH), f32),
        ),
        in_specs=[hbm] * 13,
        out_specs=(vmem, vmem),
        scratch_shapes=[
            pltpu.VMEM((1, BATCH), i32), pltpu.VMEM((1, BATCH), i32), pltpu.VMEM((1, BATCH), i32),
            pltpu.VMEM((1, rows), i32), pltpu.VMEM((1, rows), i32), pltpu.VMEM((1, rows), i32),
            pltpu.VMEM((1, WIDTH), f32), pltpu.VMEM((1, WIDTH), f32),
            dma((8,)),
            pltpu.VMEM((NODE, WIDTH), f32),
            pltpu.VMEM((WIDTH, WIDTH), bf16),
            pltpu.VMEM((WIDTH, 3 * WIDTH), bf16),
            pltpu.VMEM((WIDTH, 3 * WIDTH), bf16),
            pltpu.VMEM((BATCH, WIDTH), bf16),
            dma((5,)),
            pltpu.VMEM((Y, 2, NODE, WIDTH), bf16), dma((Y, 2)), dma((Y, 2)), dma((Y,)), dma((Y,)),
            pltpu.VMEM((X, Y, 128), f32), pltpu.VMEM((X, Y, 128), f32), dma((X,)), dma((X,)),
            pltpu.VMEM((2, NODE, WIDTH), bf16), dma((2,)), dma((2,)),
            pltpu.VMEM((Y, 2 * ROW, 128), f32), pltpu.VMEM((Y, 2 * ROW, 128), f32), dma((Y,)), dma((Y,)),
            pltpu.VMEM((ROW, 128), f32), pltpu.VMEM((ROW, ROW, 128), f32), dma((ROW,)), dma((ROW,)),
            pltpu.VMEM((Y, BLOCK, BATCH), f32),
            pltpu.VMEM((Y, BLOCK, WIDTH), f32),
            pltpu.VMEM((Y, BLOCK, 2 * BATCH), bf16),
            pltpu.VMEM((Y, BLOCK, BATCH), bf16),
            pltpu.VMEM((Y, X, 4 * SLOT, 256), bf16), pltpu.VMEM((Y, X, 4 * SLOT, 256), bf16),
            dma((Y, X)), dma((Y, X)),
            pltpu.VMEM((BATCH, WIDTH), f32), pltpu.VMEM((BATCH, WIDTH), f32), pltpu.VMEM((BATCH, 128), f32),
            pltpu.VMEM((Y * 128, 4 * BATCH), bf16),
            pltpu.VMEM((NODE, ROW * 128), bf16),
            pltpu.VMEM((2, WIDTH, 256), bf16),
            pltpu.VMEM((Y, ROW, 16, 128), bf16), pltpu.VMEM((ROW, Y, 16, 128), bf16),
            pltpu.VMEM((ROW, Y, 16, 128), bf16),
            dma((ROW,)), dma((ROW,)), dma((Y,)), dma((Y,)),
            pltpu.VMEM((2, 2 * BATCH, 256), bf16), pltpu.VMEM((3, 2 * BATCH, WIDTH), bf16),
            dma((4,)), dma((4,)),
            pltpu.VMEM((3, 192, WIDTH), bf16), pltpu.VMEM((3, X, 64, WIDTH), bf16), dma((3, X)), dma((3, X)),
            pltpu.VMEM((3, Y, 16, 256), bf16), pltpu.VMEM((3, Y, 16, 256), bf16), dma((3, Y)), dma((3, Y)),
            pltpu.VMEM((3, Z, 16, 256), bf16), dma((3, Z)), dma((3, Z)),
        ],
        compiler_params=pltpu.CompilerParams(
            collective_id=0, has_side_effects=True, vmem_limit_bytes=60 * 2**20
        ),
        cost_estimate=pl.CostEstimate(flops=4 * 10**9, bytes_accessed=6 * 10**6, transcendentals=2 * 10**6),
    )(
        batch_owner.reshape(1, BATCH), batch_row, batch_time,
        neighbour_owner.reshape(1, rows), neighbour_row, neighbour_time,
        frequency.reshape(1, WIDTH), phase_shift.reshape(1, WIDTH),
        owned, w_message, w_input, w_recur, cotangent.reshape(BATCH, WIDTH),
    )
    return (owned + change)[None], grad[0] + grad[1]


def solution(mesh):
    return jax.shard_map(
        body,
        mesh=mesh,
        in_specs=(
            P("group", "mem", None),
            P("group", "mem", None),
            P("group", "mem"),
            P("group", "mem"),
            P("group", "mem", None),
            P("group", "mem"),
            P("group", "mem"),
            P(),
            P(),
            P(),
            P(),
            P(),
            P("group", "mem", None),
        ),
        out_specs=(P("group", "mem", None), P("mem", None)),
        check_vma=False,
    )
```

profile of v0, /device:TPU:8, one launch (start us, length us, event | category | flops | bytes accessed | tf_op | source)
XLA Modules:
  0.0 81.4 jit_solution(5306441906241628915)
XLA Ops:
  0.6 0.0 copy-start
  0.6 78.2 %shard_map.140 = (f32[256,512]{1,0:T(8,128)}, f32[2,8,1536]{2,1,0:T(8,128)}) custom-call(s32[1,128]{1,0:T(1,128)} %bitcast.16, s32[1,128]{1,0:T(1,128)} %br_hbm.1, s32[1,128]{1,0:T(1,128)} %bt_hbm.1, s32[1,1280]{1,0:T(1,128)} %bitcast.13, s32[1,1280]{1,0:T(1,128)} %nr_hbm.1, s32[1,1280]{1,0:T(1,128)} %nt_hbm.1, f32[1,512]{1,0:T(1,128)} %bitcast.14, ...), custom_call_target="tpu_custom_call" | custom-call | flops 4000000000 | bytes 6000000 | tf_op jit(solution)/shard_map/pallas_call | solution.py:532
  78.8 0.0 copy-start.1
  78.8 0.0 copy-done
  78.8 1.9 %add_bitcast_fusion = f32[1,256,512]{2,1,0:T(8,128)} fusion(f32[256,512]{1,0:T(8,128)} %get-tuple-element.4, f32[1,256,512]{2,1,0:T(8,128)S(1)} %copy-done), kind=kLoop, calls=%fused_computation | loop fusion | flops 131072 | bytes 1572864 | tf_op jit(solution)/shard_map/broadcast_in_dim | solution.py:585
  80.8 0.0 copy-done.1
  80.8 0.6 add_bitcast_fusion.1
Async XLA Ops:
  0.6 78.2 %copy-start = (f32[1,256,512]{2,1,0:T(8,128)S(1)}, f32[1,256,512]{2,1,0:T(8,128)}, u32[]{:S(2)}) copy-start(f32[1,256,512]{2,1,0:T(8,128)} %param.13) | copy-start | bytes 1572868
  78.8 2.0 %copy-start.1 = (f32[2,8,1536]{2,1,0:T(8,128)S(1)}, f32[2,8,1536]{2,1,0:T(8,128)}, u32[]{:S(2)}) copy-start(f32[2,8,1536]{2,1,0:T(8,128)} %get-tuple-element.5) | copy-start | bytes 294916
where the time goes:
time: 81.6 us; the launch traced here: 81.4 us
  Pallas kernels  78.2 us (96%)
  other arithmetic  2.57 us (3%)
    pallas_call x1, Pallas kernels, body(): pl.pallas_call(kernel, out_shape=(jax.ShapeDtypeStruct((NODE, WIDTH), f32...  78.2 us
    broadcast_in_dim x1, other arithmetic, body(): return ((owned + change)[None], grad[0] + grad[1])  1.95 us

commit v1 on v0

--- a/solution.py
+++ b/solution.py
@@ -387,12 +387,12 @@
     hand_on(3)
     serve(Y - 3)
     serve(3)
+    serve_far()
     prepare(2)
     prepare(Y - 3)
     arrived(4, 0)
     arrived(4, 1)
     hand_on(4)
-    serve_far()
     serve(4)
 
     prepare(3)

time: 81.6 us -> 80.2 us (0.983)
  the two profiles are of different devices: /device:TPU:8 before, /device:TPU:2 now
where the time goes in v1:
time: 80.2 us; the launch traced here: 80 us
  Pallas kernels  76.8 us (96%)
  other arithmetic  2.57 us (3%)
    pallas_call x1, Pallas kernels, body(): pl.pallas_call(kernel, out_shape=(jax.ShapeDtypeStruct((NODE, WIDTH), f32...  76.8 us
    broadcast_in_dim x1, other arithmetic, body(): return ((owned + change)[None], grad[0] + grad[1])  1.95 us

profile of v1, /device:TPU:2, one launch (start us, length us, event | category | flops | bytes accessed | tf_op | source)
XLA Modules:
  0.0 80.0 jit_solution(1318551487837750013)
XLA Ops:
  0.6 0.0 copy-start
  0.6 76.8 %shard_map.140 = (f32[256,512]{1,0:T(8,128)}, f32[2,8,1536]{2,1,0:T(8,128)}) custom-call(s32[1,128]{1,0:T(1,128)} %bitcast.16, s32[1,128]{1,0:T(1,128)} %br_hbm.1, s32[1,128]{1,0:T(1,128)} %bt_hbm.1, s32[1,1280]{1,0:T(1,128)} %bitcast.13, s32[1,1280]{1,0:T(1,128)} %nr_hbm.1, s32[1,1280]{1,0:T(1,128)} %nt_hbm.1, f32[1,512]{1,0:T(1,128)} %bitcast.14, ...), custom_call_target="tpu_custom_call" | custom-call | flops 4000000000 | bytes 6000000 | tf_op jit(solution)/shard_map/pallas_call | solution.py:532
  77.4 0.0 copy-start.1
  77.5 0.0 copy-done
  77.5 1.9 %add_bitcast_fusion = f32[1,256,512]{2,1,0:T(8,128)} fusion(f32[256,512]{1,0:T(8,128)} %get-tuple-element.4, f32[1,256,512]{2,1,0:T(8,128)S(1)} %copy-done), kind=kLoop, calls=%fused_computation | loop fusion | flops 131072 | bytes 1572864 | tf_op jit(solution)/shard_map/broadcast_in_dim | solution.py:585
  79.4 0.0 copy-done.1
  79.4 0.6 add_bitcast_fusion.1
Async XLA Ops:
  0.6 76.8 %copy-start = (f32[1,256,512]{2,1,0:T(8,128)S(1)}, f32[1,256,512]{2,1,0:T(8,128)}, u32[]{:S(2)}) copy-start(f32[1,256,512]{2,1,0:T(8,128)} %param.13) | copy-start | bytes 1572868
  77.4 2.0 %copy-start.1 = (f32[2,8,1536]{2,1,0:T(8,128)S(1)}, f32[2,8,1536]{2,1,0:T(8,128)}, u32[]{:S(2)}) copy-start(f32[2,8,1536]{2,1,0:T(8,128)} %get-tuple-element.5) | copy-start | bytes 294916
